TPU v7x, 32 devices: a whole 2x2x4 slice. The times are simulated.
32 devices in a mesh: seq: 2 (over y), ctx: 4 (over x, core), wt: 4 (over z).
Axes of the slice: x: 2, y: 2, z: 4, core: 2. Of those that a mesh axis runs over, the one named last changes fastest.
Arguments:
- tokens: bfloat16 [16, 1024, 768], P(('seq', 'wt'), 'ctx'), may hold values from -6 to 6
- cotangent: bfloat16 [16, 1024, 768], P(('seq', 'wt'), 'ctx'), may hold values from -6 to 6
- segment_ids: int32 [16, 1024], P(('seq', 'wt'), 'ctx'), may hold values from 0 to 4, as said below
- lengths: int32 [16, 4], P(('seq', 'wt')), may hold values from 32 to 928, as said below
- w_query: bfloat16 [768, 768], P('wt'), may hold values from -0.21875 to 0.21875
- b_query: bfloat16 [768], P('wt'), may hold values from -3 to 3
- w_key: bfloat16 [768, 768], P('wt'), may hold values from -0.21875 to 0.21875
- w_value: bfloat16 [768, 768], P('wt'), may hold values from -0.21875 to 0.21875
- b_value: bfloat16 [768], P('wt'), may hold values from -3 to 3
- w_attn: bfloat16 [768, 768], P('wt'), may hold values from -1.75 to 1.75
- b_attn: bfloat16 [768], P('wt'), may hold values from -2 to 2
- ln1_gain: bfloat16 [768], P('wt'), may hold values from 0.5 to 1.5
- ln1_shift: bfloat16 [768], P('wt'), may hold values from -2 to 2
- w_inner: bfloat16 [768, 3072], P('wt'), may hold values from -0.21875 to 0.21875
- b_inner: bfloat16 [3072], P('wt'), may hold values from -3 to 3
- w_outer: bfloat16 [3072, 768], P('wt'), may hold values from -0.109375 to 0.109375
- b_outer: bfloat16 [768], P('wt'), may hold values from -2 to 2
- ln2_gain: bfloat16 [768], P('wt'), may hold values from 0.5 to 1.5
- ln2_shift: bfloat16 [768], P('wt'), may hold values from -2 to 2
Outputs:
- layer_out: bfloat16 [16, 1024, 768], P(('seq', 'wt'), 'ctx')
- grad_input: bfloat16 [16, 1024, 768], P(('seq', 'wt'), 'ctx')
- grad_w_query: float32 [768, 768], P('wt')
- grad_b_query: float32 [768], P('wt')
- grad_w_key: float32 [768, 768], P('wt')
- grad_w_value: float32 [768, 768], P('wt')
- grad_b_value: float32 [768], P('wt')
- grad_w_attn: float32 [768, 768], P('wt')
- grad_b_attn: float32 [768], P('wt')
- grad_ln1_gain: float32 [768], P('wt')
- grad_ln1_shift: float32 [768], P('wt')
- grad_w_inner: float32 [768, 3072], P('wt')
- grad_b_inner: float32 [3072], P('wt')
- grad_w_outer: float32 [3072, 768], P('wt')
- grad_b_outer: float32 [768], P('wt')
- grad_ln2_gain: float32 [768], P('wt')
- grad_ln2_shift: float32 [768], P('wt')
Inputs may be any that keep to these rules, and one draw needn't show every extreme that they name: `lengths`: the 4 documents of a sequence lie end to end from its first position, and the positions after them are padding; among the 2 sequences that one device holds, one has a single document of 1024 - 3 * max(1, 32) positions, at a place among its documents that varies, and its other documents have max(1, 32) positions each; every other sequence has documents of 64 to 256 positions. `segment_ids`: position t holds d + 1 where it lies in the sequence's document d (counted from 0 in the order of lengths), and 0 in the padding.
All inputs are finite; a program needn't handle non-finite values.
Results may differ from a plain program's by a relative error of at most 0.02.
Values may be sent and summed in bfloat16 or wider, within the bound.
No kernel may reach another device: no remote copies, remote signals or barrier semaphores. Data moves between devices by JAX's collectives and lax.ppermute only.
A program may use at most 320 MiB of HBM per device.

v0:
```python
import math
import jax
import jax.numpy as jnp
from jax import lax
from jax.sharding import PartitionSpec as P

H = 12
HD = 64
NEG = -1000000000.0
EPS = 1e-05


def product(former, latter):
    return jnp.dot(former, latter, preferred_element_type=jnp.float32)


def over_rows(former, latter):
    return lax.dot_general(
        former, latter, (((0,), (0,)), ((), ())), preferred_element_type=jnp.float32
    )


def against(former, latter):
    return lax.dot_general(
        former, latter, (((1,), (1,)), ((), ())), preferred_element_type=jnp.float32
    )


def norm_rows(values, gain, shift):
    center = jnp.mean(values, axis=-1, keepdims=True)
    offset = values - center
    spread = jnp.mean(offset * offset, axis=-1, keepdims=True)
    return offset * lax.rsqrt(spread + EPS) * gain + shift


def exact_gelu(values):
    return jax.nn.gelu(values, approximate=False)


def key_segments(doc_lens, length):
    doc_ends = jnp.cumsum(doc_lens, axis=-1)
    places = jnp.arange(length, dtype=jnp.int32)
    passed = jnp.sum((places[None, :, None] >= doc_ends[:, None, :]).astype(jnp.int32), axis=-1)
    return jnp.where(places[None, :] < doc_ends[:, -1:], passed + 1, 0)


def to_items(matrix, groups):
    seq_count, length, model_width = matrix.shape
    per_group = model_width // (groups * HD)
    shaped = matrix.reshape(seq_count, length, groups, per_group, HD)
    return shaped.transpose(0, 2, 3, 1, 4).reshape(seq_count * groups, per_group, length, HD)


def from_items(blocks, seq_count):
    count_items, per_group, length, head_size = blocks.shape
    groups = count_items // seq_count
    shaped = blocks.reshape(seq_count, groups, per_group, length, head_size)
    return shaped.transpose(0, 3, 1, 2, 4).reshape(
        seq_count, length, groups * per_group * head_size
    )


def masked_scores(head_q, head_k, q_seg, k_seg, factor):
    scores = jnp.einsum("hqd,hkd->hqk", head_q, head_k, preferred_element_type=jnp.float32) * factor
    matching = q_seg[:, None] == k_seg[None, :]
    return jnp.where(matching[None], scores, NEG)


def body(
    tokens,
    cotangent,
    segment_ids,
    lengths,
    w_query,
    b_query,
    w_key,
    w_value,
    b_value,
    w_attn,
    b_attn,
    ln1_gain,
    ln1_shift,
    w_inner,
    b_inner,
    w_outer,
    b_outer,
    ln2_gain,
    ln2_shift,
):
    shards = (
        w_query,
        b_query,
        w_key,
        w_value,
        b_value,
        w_attn,
        b_attn,
        ln1_gain,
        ln1_shift,
        w_inner,
        b_inner,
        w_outer,
        b_outer,
        ln2_gain,
        ln2_shift,
    )
    seq_count, shard_len, model_width = tokens.shape
    row_count = seq_count * shard_len
    groups = H // math.gcd(H, 4)
    factor = 1.0 / math.sqrt(HD)
    full = (
        lax.all_gather(shards[0], "wt", axis=0, tiled=True),
        lax.all_gather(shards[1], "wt", axis=0, tiled=True),
        lax.all_gather(shards[2], "wt", axis=0, tiled=True),
        lax.all_gather(shards[3], "wt", axis=0, tiled=True),
        lax.all_gather(shards[4], "wt", axis=0, tiled=True),
        lax.all_gather(shards[5], "wt", axis=0, tiled=True),
        lax.all_gather(shards[6], "wt", axis=0, tiled=True),
        lax.all_gather(shards[7], "wt", axis=0, tiled=True),
        lax.all_gather(shards[8], "wt", axis=0, tiled=True),
        lax.all_gather(shards[9], "wt", axis=0, tiled=True),
        lax.all_gather(shards[10], "wt", axis=0, tiled=True),
        lax.all_gather(shards[11], "wt", axis=0, tiled=True),
        lax.all_gather(shards[12], "wt", axis=0, tiled=True),
        lax.all_gather(shards[13], "wt", axis=0, tiled=True),
        lax.all_gather(shards[14], "wt", axis=0, tiled=True),
    )
    rows = tokens.reshape(row_count, model_width)
    query = (product(rows, full[0]) + full[1].astype(jnp.float32)).astype(jnp.bfloat16)
    key_rows = product(rows, full[2]).astype(jnp.bfloat16)
    value_rows = (product(rows, full[3]) + full[4].astype(jnp.float32)).astype(jnp.bfloat16)
    local_kv = (
        key_rows.reshape(seq_count, shard_len, model_width),
        value_rows.reshape(seq_count, shard_len, model_width),
    )
    whole_kv = (
        lax.all_gather(local_kv[0], "ctx", axis=1, tiled=True),
        lax.all_gather(local_kv[1], "ctx", axis=1, tiled=True),
    )
    seq_len = whole_kv[0].shape[1]
    key_segs = jnp.repeat(key_segments(lengths, seq_len), groups, axis=0)
    query_segs = jnp.repeat(segment_ids, groups, axis=0)
    query_items = to_items(query.reshape(seq_count, shard_len, model_width), groups)
    key_items = to_items(whole_kv[0], groups)
    value_items = to_items(whole_kv[1], groups)

    def attend(item):
        head_q, head_k, head_v, q_seg, k_seg = item
        scores = masked_scores(head_q, head_k, q_seg, k_seg, factor)
        highest = jnp.max(scores, axis=-1, keepdims=True)
        totals = jnp.sum(jnp.exp(scores - highest), axis=-1, keepdims=True)
        log_sum = highest + jnp.log(totals)
        probs = jnp.exp(scores - log_sum).astype(jnp.bfloat16)
        mixed = jnp.einsum("hqk,hkd->hqd", probs, head_v, preferred_element_type=jnp.float32)
        return (mixed, log_sum[..., 0])

    attn_items, log_sums = lax.map(
        attend, (query_items, key_items, value_items, query_segs, key_segs)
    )
    attn = from_items(attn_items, seq_count).reshape(row_count, model_width).astype(jnp.bfloat16)
    first_sum = rows.astype(jnp.float32) + product(attn, full[5]) + full[6].astype(jnp.float32)
    hidden, first_pull = jax.vjp(
        norm_rows, first_sum, full[7].astype(jnp.float32), full[8].astype(jnp.float32)
    )
    hidden_low = hidden.astype(jnp.bfloat16)
    inner = product(hidden_low, full[9]) + full[10].astype(jnp.float32)
    active, gelu_pull = jax.vjp(exact_gelu, inner)
    active_low = active.astype(jnp.bfloat16)
    second_sum = hidden + product(active_low, full[11]) + full[12].astype(jnp.float32)
    result, second_pull = jax.vjp(
        norm_rows, second_sum, full[13].astype(jnp.float32), full[14].astype(jnp.float32)
    )
    layer_out = result.astype(jnp.bfloat16).reshape(tokens.shape)
    back = (
        lax.all_gather(shards[0], "wt", axis=0, tiled=True),
        lax.all_gather(shards[1], "wt", axis=0, tiled=True),
        lax.all_gather(shards[2], "wt", axis=0, tiled=True),
        lax.all_gather(shards[3], "wt", axis=0, tiled=True),
        lax.all_gather(shards[4], "wt", axis=0, tiled=True),
        lax.all_gather(shards[5], "wt", axis=0, tiled=True),
        lax.all_gather(shards[6], "wt", axis=0, tiled=True),
        lax.all_gather(shards[7], "wt", axis=0, tiled=True),
        lax.all_gather(shards[8], "wt", axis=0, tiled=True),
        lax.all_gather(shards[9], "wt", axis=0, tiled=True),
        lax.all_gather(shards[10], "wt", axis=0, tiled=True),
        lax.all_gather(shards[11], "wt", axis=0, tiled=True),
        lax.all_gather(shards[12], "wt", axis=0, tiled=True),
        lax.all_gather(shards[13], "wt", axis=0, tiled=True),
        lax.all_gather(shards[14], "wt", axis=0, tiled=True),
    )
    back_kv = (
        lax.all_gather(local_kv[0], "ctx", axis=1, tiled=True),
        lax.all_gather(local_kv[1], "ctx", axis=1, tiled=True),
    )
    back_keys = to_items(back_kv[0], groups)
    back_values = to_items(back_kv[1], groups)
    live = (segment_ids != 0).astype(jnp.float32).reshape(row_count, 1)
    grad_rows = cotangent.reshape(row_count, model_width).astype(jnp.float32) * live
    d_second, d_gain_two, d_shift_two = second_pull(grad_rows)
    d_outer = d_second.astype(jnp.bfloat16)
    g_w_outer = over_rows(active_low, d_outer)
    g_b_outer = jnp.sum(d_outer.astype(jnp.float32), axis=0)
    d_inner = gelu_pull(against(d_outer, back[11]))[0].astype(jnp.bfloat16)
    g_w_inner = over_rows(hidden_low, d_inner)
    g_b_inner = jnp.sum(d_inner.astype(jnp.float32), axis=0)
    d_hidden = d_second + against(d_inner, back[9])
    d_first, d_gain_one, d_shift_one = first_pull(d_hidden)
    d_proj = d_first.astype(jnp.bfloat16)
    g_w_attn = over_rows(attn, d_proj)
    g_b_attn = jnp.sum(d_proj.astype(jnp.float32), axis=0)
    d_attn = against(d_proj, back[5]).astype(jnp.bfloat16)
    d_attn_seq = d_attn.reshape(seq_count, shard_len, model_width)
    d_items = to_items(d_attn_seq, groups)

    def attend_back(item):
        head_q, head_k, head_v, q_seg, k_seg, log_sum, head_d = item
        scores = masked_scores(head_q, head_k, q_seg, k_seg, factor)
        probs = jnp.exp(scores - log_sum[..., None])
        d_probs = jnp.einsum("hqd,hkd->hqk", head_d, head_v, preferred_element_type=jnp.float32)
        center = jnp.sum(probs * d_probs, axis=-1, keepdims=True)
        d_scores = (probs * (d_probs - center)).astype(jnp.bfloat16)
        d_vals = jnp.einsum(
            "hqk,hqd->hkd", probs.astype(jnp.bfloat16), head_d, preferred_element_type=jnp.float32
        )
        d_q = (
            jnp.einsum("hqk,hkd->hqd", d_scores, head_k, preferred_element_type=jnp.float32)
            * factor
        )
        d_k = (
            jnp.einsum("hqk,hqd->hkd", d_scores, head_q, preferred_element_type=jnp.float32)
            * factor
        )
        return (d_q, d_k, d_vals)

    dq_items, dk_items, dv_items = lax.map(
        attend_back, (query_items, back_keys, back_values, query_segs, key_segs, log_sums, d_items)
    )
    d_query = from_items(dq_items, seq_count).reshape(row_count, model_width).astype(jnp.bfloat16)
    partial_kv = (from_items(dk_items, seq_count), from_items(dv_items, seq_count))
    own_kv = (
        lax.psum_scatter(
            partial_kv[0].astype(jnp.bfloat16), "ctx", scatter_dimension=1, tiled=True
        ).astype(jnp.float32),
        lax.psum_scatter(
            partial_kv[1].astype(jnp.bfloat16), "ctx", scatter_dimension=1, tiled=True
        ).astype(jnp.float32),
    )
    d_key = own_kv[0].reshape(row_count, model_width).astype(jnp.bfloat16)
    d_value = own_kv[1].reshape(row_count, model_width).astype(jnp.bfloat16)
    g_w_query = over_rows(rows, d_query)
    g_b_query = jnp.sum(d_query.astype(jnp.float32), axis=0)
    g_w_key = over_rows(rows, d_key)
    g_w_value = over_rows(rows, d_value)
    g_b_value = jnp.sum(d_value.astype(jnp.float32), axis=0)
    input_sum = (
        d_first + against(d_query, back[0]) + against(d_key, back[2]) + against(d_value, back[3])
    )
    grad_input = input_sum.astype(jnp.bfloat16).reshape(tokens.shape)
    grads = (
        g_w_query,
        g_b_query,
        g_w_key,
        g_w_value,
        g_b_value,
        g_w_attn,
        g_b_attn,
        d_gain_one,
        d_shift_one,
        g_w_inner,
        g_b_inner,
        g_w_outer,
        g_b_outer,
        d_gain_two,
        d_shift_two,
    )
    shares = (
        lax.psum_scatter(
            grads[0].astype(jnp.bfloat16), "wt", scatter_dimension=0, tiled=True
        ).astype(jnp.float32),
        lax.psum_scatter(
            grads[1].astype(jnp.bfloat16), "wt", scatter_dimension=0, tiled=True
        ).astype(jnp.float32),
        lax.psum_scatter(
            grads[2].astype(jnp.bfloat16), "wt", scatter_dimension=0, tiled=True
        ).astype(jnp.float32),
        lax.psum_scatter(
            grads[3].astype(jnp.bfloat16), "wt", scatter_dimension=0, tiled=True
        ).astype(jnp.float32),
        lax.psum_scatter(
            grads[4].astype(jnp.bfloat16), "wt", scatter_dimension=0, tiled=True
        ).astype(jnp.float32),
        lax.psum_scatter(
            grads[5].astype(jnp.bfloat16), "wt", scatter_dimension=0, tiled=True
        ).astype(jnp.float32),
        lax.psum_scatter(
            grads[6].astype(jnp.bfloat16), "wt", scatter_dimension=0, tiled=True
        ).astype(jnp.float32),
        lax.psum_scatter(
            grads[7].astype(jnp.bfloat16), "wt", scatter_dimension=0, tiled=True
        ).astype(jnp.float32),
        lax.psum_scatter(
            grads[8].astype(jnp.bfloat16), "wt", scatter_dimension=0, tiled=True
        ).astype(jnp.float32),
        lax.psum_scatter(
            grads[9].astype(jnp.bfloat16), "wt", scatter_dimension=0, tiled=True
        ).astype(jnp.float32),
        lax.psum_scatter(
            grads[10].astype(jnp.bfloat16), "wt", scatter_dimension=0, tiled=True
        ).astype(jnp.float32),
        lax.psum_scatter(
            grads[11].astype(jnp.bfloat16), "wt", scatter_dimension=0, tiled=True
        ).astype(jnp.float32),
        lax.psum_scatter(
            grads[12].astype(jnp.bfloat16), "wt", scatter_dimension=0, tiled=True
        ).astype(jnp.float32),
        lax.psum_scatter(
            grads[13].astype(jnp.bfloat16), "wt", scatter_dimension=0, tiled=True
        ).astype(jnp.float32),
        lax.psum_scatter(
            grads[14].astype(jnp.bfloat16), "wt", scatter_dimension=0, tiled=True
        ).astype(jnp.float32),
    )
    summed = (
        lax.psum(shares[0].astype(jnp.bfloat16), ("seq", "ctx")).astype(jnp.float32),
        lax.psum(shares[1].astype(jnp.bfloat16), ("seq", "ctx")).astype(jnp.float32),
        lax.psum(shares[2].astype(jnp.bfloat16), ("seq", "ctx")).astype(jnp.float32),
        lax.psum(shares[3].astype(jnp.bfloat16), ("seq", "ctx")).astype(jnp.float32),
        lax.psum(shares[4].astype(jnp.bfloat16), ("seq", "ctx")).astype(jnp.float32),
        lax.psum(shares[5].astype(jnp.bfloat16), ("seq", "ctx")).astype(jnp.float32),
        lax.psum(shares[6].astype(jnp.bfloat16), ("seq", "ctx")).astype(jnp.float32),
        lax.psum(shares[7].astype(jnp.bfloat16), ("seq", "ctx")).astype(jnp.float32),
        lax.psum(shares[8].astype(jnp.bfloat16), ("seq", "ctx")).astype(jnp.float32),
        lax.psum(shares[9].astype(jnp.bfloat16), ("seq", "ctx")).astype(jnp.float32),
        lax.psum(shares[10].astype(jnp.bfloat16), ("seq", "ctx")).astype(jnp.float32),
        lax.psum(shares[11].astype(jnp.bfloat16), ("seq", "ctx")).astype(jnp.float32),
        lax.psum(shares[12].astype(jnp.bfloat16), ("seq", "ctx")).astype(jnp.float32),
        lax.psum(shares[13].astype(jnp.bfloat16), ("seq", "ctx")).astype(jnp.float32),
        lax.psum(shares[14].astype(jnp.bfloat16), ("seq", "ctx")).astype(jnp.float32),
    )
    return (layer_out, grad_input) + tuple(summed)


def solution(mesh):
    in_specs = (
        P(("seq", "wt"), "ctx", None),
        P(("seq", "wt"), "ctx", None),
        P(("seq", "wt"), "ctx"),
        P(("seq", "wt"), None),
        P("wt", None),
        P("wt"),
        P("wt", None),
        P("wt", None),
        P("wt"),
        P("wt", None),
        P("wt"),
        P("wt"),
        P("wt"),
        P("wt", None),
        P("wt"),
        P("wt", None),
        P("wt"),
        P("wt"),
        P("wt"),
    )
    out_specs = (
        P(("seq", "wt"), "ctx", None),
        P(("seq", "wt"), "ctx", None),
        P("wt", None),
        P("wt"),
        P("wt", None),
        P("wt", None),
        P("wt"),
        P("wt", None),
        P("wt"),
        P("wt"),
        P("wt"),
        P("wt", None),
        P("wt"),
        P("wt", None),
        P("wt"),
        P("wt"),
        P("wt"),
    )
    return jax.shard_map(body, mesh=mesh, in_specs=in_specs, out_specs=out_specs, check_vma=False)
```

profile of v0, /device:TPU:0, one launch (start us, length us, event | category | flops | bytes accessed | tf_op | source)
XLA Modules:
  0.0 968.8 jit_solution(11220610871833606484)
XLA Ops:
  17.3 21.1 %all-reduce.20 = (bf16[768]{0:T(1024)(128)(2,1)S(1)}, bf16[768]{0:T(1024)(128)(2,1)S(1)}, bf16[768]{0:T(1024)(128)(2,1)S(1)}, bf16[768]{0:T(1024)(128)(2,1)S(1)}...) all-reduce(bf16[768]{0:T(1024)(128)(2,1)S(1)} %dynamic-update-slice, ...), channel_id=1, replica_groups=mesh['seq'=2,'ctx'=4,'wt'=4] {'wt'}, use_global_device_ids=true, to_apply=%add | all-reduce | flops 5376 | bytes 21504
  46.9 27.5 %all-gather.12.cloned.1.call-done = bf16[768,768]{1,0:T(8,128)(2,1)} async-done(((bf16[192,768]{1,0:T(8,128)(2,1)}), bf16[768,768]{1,0:T(8,128)(2,1)}) %all-gather.12.cloned.1.call-update) | async-done | bytes 1179664 | tf_op jit(solution)/shard_map/all_gather | solution.py:114
  81.1 13.6 %all-gather = bf16[4,1,768]{2,1,0:T(2,128)(2,1)S(1)} all-gather(bf16[1,1,768]{2,1,0:T(2,128)(2,1)S(1)} %reshape.309), channel_id=1, replica_groups=mesh['seq'=2,'ctx'=4,'wt'=4] {'wt'}, dimensions={0}, use_global_device_ids=true | all-gather | bytes 7680 | tf_op jit(solution)/shard_map/all_gather | solution.py:122
  94.7 11.1 %all-gather.10.cloned.1.call-done = bf16[768,768]{1,0:T(8,128)(2,1)} async-done(((bf16[192,768]{1,0:T(8,128)(2,1)}), bf16[768,768]{1,0:T(8,128)(2,1)}) %all-gather.10.cloned.1.call-update) | async-done | bytes 1179664 | tf_op jit(solution)/shard_map/all_gather | solution.py:112
  108.5 27.4 %all-gather.18.cloned.1.call-done = bf16[2,1024,768]{1,2,0:T(8,128)(2,1)} async-done(((bf16[2,256,768]{1,2,0:T(8,128)(2,1)}), bf16[2,1024,768]{1,2,0:T(8,128)(2,1)}) %all-gather.18.cloned.1.call-update) | async-done | bytes 3145744 | tf_op jit(solution)/shard_map/all_gather | solution.py:138
  135.8 30.9 %all-gather.14.cloned.1.call-done = bf16[2,1024,768]{1,2,0:T(8,128)(2,1)} async-done(((bf16[2,256,768]{1,2,0:T(8,128)(2,1)}), bf16[2,1024,768]{1,2,0:T(8,128)(2,1)}) %all-gather.14.cloned.1.call-update) | async-done | bytes 3145744 | tf_op jit(solution)/shard_map/all_gather | solution.py:137
  166.9 34.3 %while.26 = (s32[]{:T(128)}, bf16[6,4,256,64]{2,3,1,0:T(8,128)(2,1)S(1)}, f32[6,4,256]{2,1,0:T(4,128)S(1)}, s32[6,256]{1,0:T(8,128)S(1)}, s32[6,1024]{1,0:T(8,12...) while((s32[]{:T(128)}, ...), condition=%wide.region_5.6_spmd, body=%wide.region_2.5_spmd.sunk | while | flops 280230912 | bytes 15123561 | solution.py:157
  205.2 83.6 %all-gather.22.cloned.1.call-done = bf16[768,3072]{1,0:T(8,128)(2,1)} async-done(((bf16[192,3072]{1,0:T(8,128)(2,1)}), bf16[768,3072]{1,0:T(8,128)(2,1)}) %all-gather.22.cloned.1.call-update) | async-done | bytes 4718608 | tf_op jit(solution)/shard_map/all_gather | solution.py:121
  288.8 19.8 %multiply_convert_fusion.1 = (bf16[512,3072]{1,0:T(8,128)(2,1)}, f32[512,3072]{1,0:T(8,128)}, f32[512,3072]{1,0:T(8,128)}) fusion(f32[3072]{0:T(1024)S(1)} %bitcast.251, bf16[768,3072]{1,0:T(8,128)(2,1)} %all-gather.22.cloned.1.call-done, f32[512,768]{1,0:T(8,128)S(1)} %get-tuple-element.307, f32[768]{0:T(1024)S(1)} %convert_element_type.289, ...), kind=kOutput, calls=%fused_computation.68 | convolution fusion | flops 2521694208 | bytes 22042624 | tf_op jit(solution)/shard_map/dot_general | solution.py:14
  308.6 69.7 %all-gather.24.cloned.1.call-done = bf16[3072,768]{1,0:T(8,128)(2,1)} async-done(((bf16[768,768]{1,0:T(8,128)(2,1)}), bf16[3072,768]{1,0:T(8,128)(2,1)}) %all-gather.24.cloned.1.call-update) | async-done | bytes 4718608 | tf_op jit(solution)/shard_map/all_gather | solution.py:123
  388.1 7.9 fusion.71
  412.5 83.7 %while.27 = (s32[]{:T(128)}, bf16[6,4,256,64]{2,3,1,0:T(8,128)(2,1)}, bf16[6,4,1024,64]{2,3,1,0:T(8,128)(2,1)}, bf16[6,4,1024,64]{2,3,1,0:T(8,128)(2,1)}, s32[6,...) while((s32[]{:T(128)}, ...), condition=%wide.region_16.17_spmd, body=%wide.region_14.16_spmd.sunk | while | flops 687406080 | bytes 37011584 | solution.py:235
  504.4 28.4 %reduce-scatter.17.cloned.1.call-done = bf16[2,256,768]{1,2,0:T(8,128)(2,1)} async-done(((bf16[2,1024,768]{1,2,0:T(8,128)(2,1)}), bf16[2,256,768]{1,2,0:T(8,128)(2,1)}) %reduce-scatter.17.cloned.1.call-update) | async-done | bytes 786448 | tf_op jit(solution)/shard_map/reduce_scatter | solution.py:244
  538.4 34.9 %reduce-scatter.15.cloned.1.call-done = bf16[2,256,768]{1,2,0:T(8,128)(2,1)} async-done(((bf16[2,1024,768]{1,2,0:T(8,128)(2,1)}), bf16[2,256,768]{1,2,0:T(8,128)(2,1)}) %reduce-scatter.15.cloned.1.call-update) | async-done | bytes 786448 | tf_op jit(solution)/shard_map/reduce_scatter | solution.py:241
  582.3 7.4 convolution_convert_fusion.1
  589.7 6.9 convolution_convert_fusion
  606.7 28.2 %reduce-scatter.29.cloned.1.call-done = bf16[192,768]{1,0:T(8,128)(2,1)} async-done(((bf16[768,768]{1,0:T(8,128)(2,1)}), bf16[192,768]{1,0:T(8,128)(2,1)}) %reduce-scatter.29.cloned.1.call-update) | async-done | bytes 294928
  636.8 28.4 %reduce-scatter.27.cloned.1.call-done = bf16[192,768]{1,0:T(8,128)(2,1)} async-done(((bf16[768,768]{1,0:T(8,128)(2,1)}), bf16[192,768]{1,0:T(8,128)(2,1)}) %reduce-scatter.27.cloned.1.call-update) | async-done | bytes 294928
  667.0 28.8 %reduce-scatter.19.cloned.1.call-done = bf16[192,768]{1,0:T(8,128)(2,1)} async-done(((bf16[768,768]{1,0:T(8,128)(2,1)}), bf16[192,768]{1,0:T(8,128)(2,1)}) %reduce-scatter.19.cloned.1.call-update) | async-done | bytes 294928 | tf_op jit(solution)/shard_map/reduce_scatter | solution.py:292
  695.8 86.2 %reduce-scatter.21.cloned.1.call-done = bf16[192,3072]{1,0:T(8,128)(2,1)} async-done(((bf16[768,3072]{1,0:T(8,128)(2,1)}), bf16[192,3072]{1,0:T(8,128)(2,1)}) %reduce-scatter.21.cloned.1.call-update) | async-done | bytes 1179664 | tf_op jit(solution)/shard_map/reduce_scatter | solution.py:304
  782.0 88.0 %reduce-scatter.23.cloned.1.call-done = bf16[768,768]{1,0:T(8,128)(2,1)} async-done(((bf16[3072,768]{1,0:T(8,128)(2,1)}), bf16[768,768]{1,0:T(8,128)(2,1)}) %reduce-scatter.23.cloned.1.call-update) | async-done | bytes 1179664 | tf_op jit(solution)/shard_map/reduce_scatter | solution.py:310
  879.3 18.2 %all-reduce.19 = (bf16[768]{0:T(1024)(128)(2,1)S(1)}, bf16[768]{0:T(1024)(128)(2,1)S(1)}, bf16[768]{0:T(1024)(128)(2,1)S(1)}, bf16[768]{0:T(1024)(128)(2,1)S(1)}...) all-reduce(bf16[768]{0:T(1024)(128)(2,1)S(1)} %dynamic-update-slice, ...), channel_id=1, replica_groups=mesh['seq'=2,'ctx'=4,'wt'=4] {'wt'}, use_global_device_ids=true, to_apply=%add.7 | all-reduce | flops 9984 | bytes 39936
  898.2 12.5 %all-reduce.17 = (bf16[192]{0:T(256)(128)(2,1)S(1)}, bf16[192]{0:T(256)(128)(2,1)S(1)}, bf16[192]{0:T(256)(128)(2,1)S(1)}, bf16[192]{0:T(256)(128)(2,1)S(1)}, bf...) all-reduce(bf16[192]{0:T(256)(128)(2,1)S(1)} %dynamic-slice.9, ...), channel_id=1, replica_groups=mesh['seq'=2,'ctx'=4,'wt'=4] {'seq','ctx'}, use_global_device_ids=true, to_apply=%region_23.24 | all-reduce | flops 2304 | bytes 9216 | tf_op jit(solution)/shard_map/psum | solution.py:325
  926.0 27.6 %all-reduce.23.cloned.1.call-done = (bf16[192,768]{0,1:T(8,128)(2,1)}, bf16[192,768]{0,1:T(8,128)(2,1)}, bf16[192,768]{0,1:T(8,128)(2,1)}, bf16[192,768]{1,0:T(8...) async-done(((bf16[192,768]{0,1:T(8,128)(2,1)}, bf16[192,768]{0,1:T(8,128)(2,1)}, bf16[192,768]{0,1:T(8,128)(2,1)}, bf16[192,768]{1,0:T(8,128)(2,1)}, ...) | async-done | bytes 3538960 | tf_op jit(solution)/shard_map/psum | solution.py:324
  (314 shorter events, 243.3 us)
Async XLA Ops:
  7.2 36.1 %all-gather.16.cloned.1.call-start = ((), (), s32[]{:S(2)}) async-start(), calls=%async_computation.11 | async-start | bytes 1474560 | tf_op jit(solution)/shard_map/all_gather | solution.py:115
  7.9 66.5 %all-gather.12.cloned.1.call-start = ((), (), s32[]{:S(2)}) async-start(), calls=%async_computation.9 | async-start | bytes 1474560 | tf_op jit(solution)/shard_map/all_gather | solution.py:114
  8.7 97.1 %all-gather.10.cloned.1.call-start = ((), (), s32[]{:S(2)}) async-start(), calls=%async_computation.8 | async-start | bytes 1474560 | tf_op jit(solution)/shard_map/all_gather | solution.py:112
  9.4 126.4 %all-gather.18.cloned.1.call-start = ((), (), s32[]{:S(2)}) async-start(), calls=%async_computation.12 | async-start | bytes 3932160 | tf_op jit(solution)/shard_map/all_gather | solution.py:138
  43.3 31.1 %copy-start.21 = (bf16[2,256,768]{2,1,0:T(8,128)(2,1)S(1)}, bf16[2,256,768]{2,1,0:T(8,128)(2,1)}, u32[]{:S(2)}) copy-start(bf16[2,256,768]{2,1,0:T(8,128)(2,1)} %param.23) | copy-start | bytes 2359300
  46.9 119.9 %all-gather.14.cloned.1.call-start = ((), (), s32[]{:S(2)}) async-start(), calls=%async_computation.10 | async-start | bytes 3932160 | tf_op jit(solution)/shard_map/all_gather | solution.py:137
  77.7 124.5 %all-gather.20.cloned.1.call-start = ((), (), s32[]{:S(2)}) async-start(), calls=%async_computation.13 | async-start | bytes 1474560 | tf_op jit(solution)/shard_map/all_gather | solution.py:117
  78.3 210.5 %all-gather.22.cloned.1.call-start = ((), (), s32[]{:S(2)}) async-start(), calls=%async_computation.14 | async-start | bytes 5898240 | tf_op jit(solution)/shard_map/all_gather | solution.py:121
  79.1 299.3 %all-gather.24.cloned.1.call-start = ((), (), s32[]{:S(2)}) async-start(), calls=%async_computation.15 | async-start | bytes 5898240 | tf_op jit(solution)/shard_map/all_gather | solution.py:123
  79.8 453.0 %reduce-scatter.17.cloned.1.call-start = ((), (), s32[]{:S(2)}) async-start(), calls=%async_computation.17 | async-start | bytes 3932160 | tf_op jit(solution)/shard_map/reduce_scatter | solution.py:244
  204.9 191.1 %copy-start.2 = (f32[512,768]{1,0:T(8,128)}, f32[512,768]{1,0:T(8,128)S(1)}, u32[]{:S(2)}) copy-start(f32[512,768]{1,0:T(8,128)S(1)} %get-tuple-element.307) | copy-start | bytes 4718596
  378.3 6.4 copy-start.1
  386.2 9.8 %slice-start = ((s8[4718592]{0:T(1024)(128)(4,1)}), s8[4194304]{0:T(1024)(128)(4,1)S(1)}, s32[]{:S(2)}) async-start(s8[4718592]{0:T(1024)(128)(4,1)} %bitcast.253), calls=%async_computation.25 | async-start | bytes 8388608
  386.4 9.6 copy-start.9
  388.1 8.0 slice-start.1
  496.2 77.0 %reduce-scatter.15.cloned.1.call-start = ((), (), s32[]{:S(2)}) async-start(), calls=%async_computation.16 | async-start | bytes 3932160 | tf_op jit(solution)/shard_map/reduce_scatter | solution.py:241
  496.8 108.0 %reduce-scatter.25.cloned.1.call-start = ((), (), s32[]{:S(2)}) async-start(), calls=%async_computation.21 | async-start | bytes 1474560
  504.3 130.6 %reduce-scatter.29.cloned.1.call-start = ((), (), s32[]{:S(2)}) async-start(), calls=%async_computation.23 | async-start | bytes 1474560
  538.3 126.8 %reduce-scatter.27.cloned.1.call-start = ((), (), s32[]{:S(2)}) async-start(), calls=%async_computation.22 | async-start | bytes 1474560
  578.8 117.0 %reduce-scatter.19.cloned.1.call-start = ((), (), s32[]{:S(2)}) async-start(), calls=%async_computation.18 | async-start | bytes 1474560 | tf_op jit(solution)/shard_map/reduce_scatter | solution.py:292
  582.1 199.9 %reduce-scatter.21.cloned.1.call-start = ((), (), s32[]{:S(2)}) async-start(), calls=%async_computation.19 | async-start | bytes 5898240 | tf_op jit(solution)/shard_map/reduce_scatter | solution.py:304
  589.7 280.3 %reduce-scatter.23.cloned.1.call-start = ((), (), s32[]{:S(2)}) async-start(), calls=%async_computation.20 | async-start | bytes 5898240 | tf_op jit(solution)/shard_map/reduce_scatter | solution.py:310
  596.7 273.3 %copy-start.15 = (f32[2,256]{1,0:T(2,128)S(1)}, f32[2,256]{1,0:T(2,128)}, u32[]{:S(2)}) copy-start(f32[2,256]{1,0:T(2,128)} %get-tuple-element.302) | copy-start | bytes 6148
  596.7 356.9 %all-reduce.23.cloned.1.call-start = ((), (), s32[]{:S(2)}) async-start(), calls=%async_computation.24 | async-start | bytes 7667712 | tf_op jit(solution)/shard_map/psum | solution.py:324
  (20 other events, 66.7 us)
Sparse Core Ops, SparseCore 0:
  9.6 33.6 all-gather.15
  44.9 29.5 all-gather.11
  76.0 29.7 all-gather.9
  107.8 28.0 all-gather.17
  137.8 28.9 all-gather.13
  168.2 30.4 all-gather.19
  200.3 88.5 all-gather.21
  290.4 87.8 all-gather.23
  496.3 36.3 reduce-scatter.16
  535.3 37.9 reduce-scatter.14
  575.6 29.1 reduce-scatter.24
  607.0 27.8 reduce-scatter.28
  637.2 27.8 reduce-scatter.26
  667.9 27.8 reduce-scatter.18
  698.0 83.9 reduce-scatter.20
  784.1 85.7 reduce-scatter.22
  874.5 79.0 all-reduce.22
where the time goes:
time: 975 us; the launch traced here: 969 us
  waiting for transfers between devices  617 us (63%)
  matrix products  181 us (19%)
  blocking collectives  65.3 us (7%)
  local copies, waits for them, and re-layouts  47.2 us (5%)
  other arithmetic  40.5 us (4%)
  between operations  16.7 us (2%)
    reduce_scatter x1, waiting for transfers between devices, body(): lax.psum_scatter(grads[11].astype(jnp.bfloat16), 'wt', scatter_dimension=...  88 us
    reduce_scatter x1, waiting for transfers between devices, body(): lax.psum_scatter(grads[9].astype(jnp.bfloat16), 'wt', scatter_dimension=0...  86.2 us
    all_gather x1, waiting for transfers between devices, body(): lax.all_gather(shards[9], 'wt', axis=0, tiled=True)  83.6 us
    all_gather x1, waiting for transfers between devices, body(): lax.all_gather(shards[11], 'wt', axis=0, tiled=True)  69.7 us
    unnamed x20, waiting for transfers between devices  67.8 us
    unnamed x2, blocking collectives  39.3 us
    dot_general x6, matrix products, product(): return jnp.dot(former, latter, preferred_element_type=jnp.float32)  35 us
    reduce_scatter x1, waiting for transfers between devices, body(): lax.psum_scatter(partial_kv[0].astype(jnp.bfloat16), 'ctx', scatter_dimen...  34.9 us
  transfers between devices with their start and end apart: 17, of which 16 were waited for; matrix products, arithmetic and copies ran while one was open for 15% of the time, Pallas kernels for 0%

commit v1 on v0

--- a/solution.py
+++ b/solution.py
@@ -8,6 +8,30 @@
 HD = 64
 NEG = -1000000000.0
 EPS = 1e-05
+
+
+def group_spot(page, pos_dim):
+    page = jnp.moveaxis(page, 0, pos_dim)
+    o_now = page.shape
+    return page.reshape(
+        *o_now[:pos_dim], o_now[pos_dim] * o_now[pos_dim + 1], *o_now[pos_dim + 2 :]
+    )
+
+
+def register_sector_over_axis(content, dev_axis):
+    item_now = jax.lax.axis_size(dev_axis)
+    part_next, plain = (item_now, jax.lax.axis_index(dev_axis))
+    odd, outer = (content[None], 1)
+    while outer < part_next:
+        big = jax.lax.ppermute(
+            odd, dev_axis, [(dev_i, dev_i ^ outer) for dev_i in range(part_next)]
+        )
+        seen_now = plain & outer == 0
+        opened = jnp.where(seen_now, odd, big)
+        e_next = jnp.where(seen_now, big, odd)
+        odd = jnp.concatenate([opened, e_next])
+        outer *= 2
+    return odd
 
 
 def product(former, latter):
@@ -133,8 +157,12 @@
         key_rows.reshape(seq_count, shard_len, model_width),
         value_rows.reshape(seq_count, shard_len, model_width),
     )
+
+    def track_the_roots(dim_i, buf, x_local):
+        return group_spot(register_sector_over_axis(x_local, buf), dim_i)
+
     whole_kv = (
-        lax.all_gather(local_kv[0], "ctx", axis=1, tiled=True),
+        track_the_roots(1, "ctx", local_kv[0]),
         lax.all_gather(local_kv[1], "ctx", axis=1, tiled=True),
     )
     seq_len = whole_kv[0].shape[1]

time: 975 us -> 946 us (0.970)
  waiting for transfers between devices: 617 us -> 566 us
  local copies, waits for them, and re-layouts: 47.2 us -> 60.1 us
    all_gather x1, waiting for transfers between devices: 30.9 us -> 0.01 us  [body(): lax.all_gather(local_kv[0], 'ctx', axis=1, tiled=True)]
    all_gather x1, waiting for transfers between devices: 27.4 us -> 7.81 us  [body(): lax.all_gather(local_kv[1], 'ctx', axis=1, tiled=True)]
    unnamed x93 -> x95, local copies, waits for them, and re-layouts: 27.9 us -> 28.2 us
  transfers between devices with their start and end apart: 17 -> 19, of which waited for: 16 -> 17; matrix products, arithmetic and copies ran while one was open for 15% -> 20% of each run, Pallas kernels for 0% -> 0%
where the time goes in v1:
time: 946 us; the launch traced here: 939 us
  waiting for transfers between devices  566 us (60%)
  matrix products  184 us (19%)
  blocking collectives  65 us (7%)
  local copies, waits for them, and re-layouts  60.1 us (6%)
  other arithmetic  43.8 us (5%)
  between operations  16.8 us (2%)
    reduce_scatter x1, waiting for transfers between devices, body(): lax.psum_scatter(grads[9].astype(jnp.bfloat16), 'wt', scatter_dimension=0...  88 us
    reduce_scatter x1, waiting for transfers between devices, body(): lax.psum_scatter(grads[11].astype(jnp.bfloat16), 'wt', scatter_dimension=...  86.2 us
    all_gather x1, waiting for transfers between devices, body(): lax.all_gather(shards[9], 'wt', axis=0, tiled=True)  78.5 us
    all_gather x1, waiting for transfers between devices, body(): lax.all_gather(shards[11], 'wt', axis=0, tiled=True)  69.6 us
    unnamed x20, waiting for transfers between devices  67.6 us
    unnamed x2, blocking collectives  39.3 us
    dot_general x6, matrix products, product(): return jnp.dot(former, latter, preferred_element_type=jnp.float32)  35.1 us
    reduce_scatter x1, waiting for transfers between devices, body(): lax.psum_scatter(partial_kv[1].astype(jnp.bfloat16), 'ctx', scatter_dimen...  34.9 us
  transfers between devices with their start and end apart: 19, of which 17 were waited for; matrix products, arithmetic and copies ran while one was open for 20% of the time, Pallas kernels for 0%

profile of v1, /device:TPU:0, one launch (start us, length us, event | category | flops | bytes accessed | tf_op | source)
XLA Modules:
  0.0 938.6 jit_solution(15649347077492127749)
XLA Ops:
  17.3 21.1 %all-reduce.20 = (bf16[768]{0:T(1024)(128)(2,1)S(1)}, bf16[768]{0:T(1024)(128)(2,1)S(1)}, bf16[768]{0:T(1024)(128)(2,1)S(1)}, bf16[768]{0:T(1024)(128)(2,1)S(1)}...) all-reduce(bf16[768]{0:T(1024)(128)(2,1)S(1)} %dynamic-update-slice, ...), channel_id=1, replica_groups=mesh['seq'=2,'ctx'=4,'wt'=4] {'wt'}, use_global_device_ids=true, to_apply=%add | all-reduce | flops 5376 | bytes 21504
  48.7 25.7 %all-gather.12.cloned.1.call-done = bf16[768,768]{1,0:T(8,128)(2,1)} async-done(((bf16[192,768]{1,0:T(8,128)(2,1)}), bf16[768,768]{1,0:T(8,128)(2,1)}) %all-gather.12.cloned.1.call-update) | async-done | bytes 1179664 | tf_op jit(solution)/shard_map/all_gather | solution.py:138
  82.4 13.3 %all-gather = bf16[4,1,768]{2,1,0:T(2,128)(2,1)S(1)} all-gather(bf16[1,1,768]{2,1,0:T(2,128)(2,1)S(1)} %reshape.311), channel_id=1, replica_groups=mesh['seq'=2,'ctx'=4,'wt'=4] {'wt'}, dimensions={0}, use_global_device_ids=true | all-gather | bytes 7680 | tf_op jit(solution)/shard_map/all_gather | solution.py:146
  96.3 9.5 %all-gather.10.cloned.1.call-done = bf16[768,768]{1,0:T(8,128)(2,1)} async-done(((bf16[192,768]{1,0:T(8,128)(2,1)}), bf16[768,768]{1,0:T(8,128)(2,1)}) %all-gather.10.cloned.1.call-update) | async-done | bytes 1179664 | tf_op jit(solution)/shard_map/all_gather | solution.py:136
  128.0 7.8 all-gather.16.cloned.1.call-done
  136.8 37.2 %while.26 = (s32[]{:T(128)}, bf16[6,4,256,64]{2,3,1,0:T(8,128)(2,1)}, f32[6,4,256]{2,1,0:T(4,128)S(1)}, s32[6,256]{1,0:T(8,128)S(1)}, s32[6,1024]{1,0:T(8,128)S(...) while((s32[]{:T(128)}, ...), condition=%wide.region_5.6_spmd, body=%wide.region_2.5_spmd.sunk | while | flops 280230912 | bytes 15123561 | solution.py:185
  179.2 78.5 %all-gather.20.cloned.1.call-done = bf16[768,3072]{1,0:T(8,128)(2,1)} async-done(((bf16[192,3072]{1,0:T(8,128)(2,1)}), bf16[768,3072]{1,0:T(8,128)(2,1)}) %all-gather.20.cloned.1.call-update) | async-done | bytes 4718608 | tf_op jit(solution)/shard_map/all_gather | solution.py:145
  257.7 19.8 %multiply_convert_fusion.1 = (bf16[512,3072]{1,0:T(8,128)(2,1)}, f32[512,3072]{1,0:T(8,128)}, f32[512,3072]{1,0:T(8,128)}) fusion(f32[3072]{0:T(1024)S(1)} %bitcast.262, bf16[768,3072]{1,0:T(8,128)(2,1)} %all-gather.20.cloned.1.call-done, f32[512,768]{1,0:T(8,128)S(1)} %get-tuple-element.311, f32[768]{0:T(1024)S(1)} %convert_element_type.289, ...), kind=kOutput, calls=%fused_computation.68 | convolution fusion | flops 2521694208 | bytes 22042624 | tf_op jit(solution)/shard_map/dot_general | solution.py:38
  277.6 69.6 %all-gather.22.cloned.1.call-done = bf16[3072,768]{1,0:T(8,128)(2,1)} async-done(((bf16[768,768]{1,0:T(8,128)(2,1)}), bf16[3072,768]{1,0:T(8,128)(2,1)}) %all-gather.22.cloned.1.call-update) | async-done | bytes 4718608 | tf_op jit(solution)/shard_map/all_gather | solution.py:147
  357.3 8.1 fusion.71
  381.9 83.7 %while.27 = (s32[]{:T(128)}, bf16[6,4,256,64]{2,3,1,0:T(8,128)(2,1)}, bf16[6,4,1024,64]{2,3,1,0:T(8,128)(2,1)}, bf16[6,4,1024,64]{2,3,1,0:T(8,128)(2,1)}, s32[6,...) while((s32[]{:T(128)}, ...), condition=%wide.region_16.17_spmd, body=%wide.region_14.16_spmd.sunk | while | flops 687406080 | bytes 37011584 | solution.py:263
  473.8 28.7 %reduce-scatter.15.cloned.1.call-done = bf16[2,256,768]{1,2,0:T(8,128)(2,1)} async-done(((bf16[2,1024,768]{1,2,0:T(8,128)(2,1)}), bf16[2,256,768]{1,2,0:T(8,128)(2,1)}) %reduce-scatter.15.cloned.1.call-update) | async-done | bytes 786448 | tf_op jit(solution)/shard_map/reduce_scatter | solution.py:269
  508.1 34.9 %reduce-scatter.17.cloned.1.call-done = bf16[2,256,768]{1,2,0:T(8,128)(2,1)} async-done(((bf16[2,1024,768]{1,2,0:T(8,128)(2,1)}), bf16[2,256,768]{1,2,0:T(8,128)(2,1)}) %reduce-scatter.17.cloned.1.call-update) | async-done | bytes 786448 | tf_op jit(solution)/shard_map/reduce_scatter | solution.py:272
  552.0 6.9 convolution_convert_fusion
  559.0 7.4 convolution_convert_fusion.1
  568.1 6.5 reduce-scatter.25.cloned.1.call-done
  576.5 28.2 %reduce-scatter.27.cloned.1.call-done = bf16[192,768]{1,0:T(8,128)(2,1)} async-done(((bf16[768,768]{1,0:T(8,128)(2,1)}), bf16[192,768]{1,0:T(8,128)(2,1)}) %reduce-scatter.27.cloned.1.call-update) | async-done | bytes 294928
  606.5 28.4 %reduce-scatter.29.cloned.1.call-done = bf16[192,768]{1,0:T(8,128)(2,1)} async-done(((bf16[768,768]{1,0:T(8,128)(2,1)}), bf16[192,768]{1,0:T(8,128)(2,1)}) %reduce-scatter.29.cloned.1.call-update) | async-done | bytes 294928
  636.8 28.8 %reduce-scatter.19.cloned.1.call-done = bf16[192,768]{1,0:T(8,128)(2,1)} async-done(((bf16[768,768]{1,0:T(8,128)(2,1)}), bf16[192,768]{1,0:T(8,128)(2,1)}) %reduce-scatter.19.cloned.1.call-update) | async-done | bytes 294928 | tf_op jit(solution)/shard_map/reduce_scatter | solution.py:320
  665.6 86.2 %reduce-scatter.23.cloned.1.call-done = bf16[768,768]{1,0:T(8,128)(2,1)} async-done(((bf16[3072,768]{1,0:T(8,128)(2,1)}), bf16[768,768]{1,0:T(8,128)(2,1)}) %reduce-scatter.23.cloned.1.call-update) | async-done | bytes 1179664 | tf_op jit(solution)/shard_map/reduce_scatter | solution.py:338
  751.7 88.0 %reduce-scatter.21.cloned.1.call-done = bf16[192,3072]{1,0:T(8,128)(2,1)} async-done(((bf16[768,3072]{1,0:T(8,128)(2,1)}), bf16[192,3072]{1,0:T(8,128)(2,1)}) %reduce-scatter.21.cloned.1.call-update) | async-done | bytes 1179664 | tf_op jit(solution)/shard_map/reduce_scatter | solution.py:332
  849.1 18.2 %all-reduce.19 = (bf16[768]{0:T(1024)(128)(2,1)S(1)}, bf16[768]{0:T(1024)(128)(2,1)S(1)}, bf16[768]{0:T(1024)(128)(2,1)S(1)}, bf16[768]{0:T(1024)(128)(2,1)S(1)}...) all-reduce(bf16[768]{0:T(1024)(128)(2,1)S(1)} %dynamic-update-slice, ...), channel_id=1, replica_groups=mesh['seq'=2,'ctx'=4,'wt'=4] {'wt'}, use_global_device_ids=true, to_apply=%add.7 | all-reduce | flops 9984 | bytes 39936
  867.9 12.5 %all-reduce.17 = (bf16[192]{0:T(256)(128)(2,1)S(1)}, bf16[192]{0:T(256)(128)(2,1)S(1)}, bf16[192]{0:T(256)(128)(2,1)S(1)}, bf16[192]{0:T(256)(128)(2,1)S(1)}, bf...) all-reduce(bf16[192]{0:T(256)(128)(2,1)S(1)} %dynamic-slice.9, ...), channel_id=1, replica_groups=mesh['seq'=2,'ctx'=4,'wt'=4] {'seq','ctx'}, use_global_device_ids=true, to_apply=%region_23.24 | all-reduce | flops 2304 | bytes 9216 | tf_op jit(solution)/shard_map/psum | solution.py:353
  895.8 27.6 %all-reduce.23.cloned.1.call-done = (bf16[192,768]{0,1:T(8,128)(2,1)}, bf16[192,768]{0,1:T(8,128)(2,1)}, bf16[192,768]{0,1:T(8,128)(2,1)}, bf16[192,768]{1,0:T(8...) async-done(((bf16[192,768]{0,1:T(8,128)(2,1)}, bf16[192,768]{0,1:T(8,128)(2,1)}, bf16[192,768]{0,1:T(8,128)(2,1)}, bf16[192,768]{1,0:T(8,128)(2,1)}, ...) | async-done | bytes 3538960 | tf_op jit(solution)/shard_map/psum | solution.py:352
  (326 shorter events, 265.5 us)
Async XLA Ops:
  7.2 36.1 %all-gather.14.cloned.1.call-start = ((), (), s32[]{:S(2)}) async-start(), calls=%async_computation.10 | async-start | bytes 1474560 | tf_op jit(solution)/shard_map/all_gather | solution.py:139
  7.9 66.5 %all-gather.12.cloned.1.call-start = ((), (), s32[]{:S(2)}) async-start(), calls=%async_computation.9 | async-start | bytes 1474560 | tf_op jit(solution)/shard_map/all_gather | solution.py:138
  8.7 97.2 %all-gather.10.cloned.1.call-start = ((), (), s32[]{:S(2)}) async-start(), calls=%async_computation.8 | async-start | bytes 1474560 | tf_op jit(solution)/shard_map/all_gather | solution.py:136
  9.4 126.4 %all-gather.16.cloned.1.call-start = ((), (), s32[]{:S(2)}) async-start(), calls=%async_computation.11 | async-start | bytes 3932160 | tf_op jit(solution)/shard_map/all_gather | solution.py:166
  45.6 28.9 %copy-start.21 = (bf16[2,256,768]{2,1,0:T(8,128)(2,1)S(1)}, bf16[2,256,768]{2,1,0:T(8,128)(2,1)}, u32[]{:S(2)}) copy-start(bf16[2,256,768]{2,1,0:T(8,128)(2,1)} %param.23) | copy-start | bytes 2359300
  46.8 129.6 %all-gather.18.cloned.1.call-start = ((), (), s32[]{:S(2)}) async-start(), calls=%async_computation.12 | async-start | bytes 1474560 | tf_op jit(solution)/shard_map/all_gather | solution.py:141
  47.4 210.3 %all-gather.20.cloned.1.call-start = ((), (), s32[]{:S(2)}) async-start(), calls=%async_computation.13 | async-start | bytes 5898240 | tf_op jit(solution)/shard_map/all_gather | solution.py:145
  48.0 299.2 %all-gather.22.cloned.1.call-start = ((), (), s32[]{:S(2)}) async-start(), calls=%async_computation.14 | async-start | bytes 5898240 | tf_op jit(solution)/shard_map/all_gather | solution.py:147
  48.7 332.3 %all-gather.24.cloned.1.call-start = ((), (), s32[]{:S(2)}) async-start(), calls=%async_computation.15 | async-start | bytes 3932160 | tf_op jit(solution)/shard_map/all_gather | solution.py:220
  76.5 2.4 collective-permute-start
  80.3 37.5 %collective-permute-start.1 = (bf16[2,2,256,768]{3,2,1,0:T(8,128)(2,1)}, bf16[2,2,256,768]{3,2,1,0:T(8,128)(2,1)}, u32[]{:S(2)}, u32[]{:S(2)}) collective-permute-start(bf16[2,2,256,768]{3,2,1,0:T(8,128)(2,1)} %pad_maximum_fusion), channel_id=1, source_target_pairs={{0,8},{4,12},{8,0},{12,4},{1,9},{5,13},{9,1},{13,5},{2,10},{6,14},... | collective-permute-start | bytes 4718600 | tf_op jit(solution)/shard_map/ppermute | solution.py:26
  112.0 390.6 %reduce-scatter.15.cloned.1.call-start = ((), (), s32[]{:S(2)}) async-start(), calls=%async_computation.16 | async-start | bytes 3932160 | tf_op jit(solution)/shard_map/reduce_scatter | solution.py:269
  178.9 186.5 %copy-start.1 = (f32[512,768]{1,0:T(8,128)}, f32[512,768]{1,0:T(8,128)S(1)}, u32[]{:S(2)}) copy-start(f32[512,768]{1,0:T(8,128)S(1)} %get-tuple-element.311) | copy-start | bytes 4718596
  355.1 10.3 %slice-start = ((s8[4718592]{0:T(1024)(128)(4,1)}), s8[4194304]{0:T(1024)(128)(4,1)S(1)}, s32[]{:S(2)}) async-start(s8[4718592]{0:T(1024)(128)(4,1)} %bitcast.264), calls=%async_computation.25 | async-start | bytes 8388608
  355.3 10.1 %copy-start.9 = (bf16[512,768]{1,0:T(8,128)(2,1)}, bf16[512,768]{1,0:T(8,128)(2,1)S(1)}, u32[]{:S(2)}) copy-start(bf16[512,768]{1,0:T(8,128)(2,1)S(1)} %get-tuple-element.287) | copy-start | bytes 2359300
  465.6 77.4 %reduce-scatter.17.cloned.1.call-start = ((), (), s32[]{:S(2)}) async-start(), calls=%async_computation.17 | async-start | bytes 3932160 | tf_op jit(solution)/shard_map/reduce_scatter | solution.py:272
  466.2 108.4 %reduce-scatter.25.cloned.1.call-start = ((), (), s32[]{:S(2)}) async-start(), calls=%async_computation.21 | async-start | bytes 1474560
  473.7 130.9 %reduce-scatter.27.cloned.1.call-start = ((), (), s32[]{:S(2)}) async-start(), calls=%async_computation.22 | async-start | bytes 1474560
  508.1 126.8 %reduce-scatter.29.cloned.1.call-start = ((), (), s32[]{:S(2)}) async-start(), calls=%async_computation.23 | async-start | bytes 1474560
  548.6 117.0 %reduce-scatter.19.cloned.1.call-start = ((), (), s32[]{:S(2)}) async-start(), calls=%async_computation.18 | async-start | bytes 1474560 | tf_op jit(solution)/shard_map/reduce_scatter | solution.py:320
  551.8 199.9 %reduce-scatter.23.cloned.1.call-start = ((), (), s32[]{:S(2)}) async-start(), calls=%async_computation.20 | async-start | bytes 5898240 | tf_op jit(solution)/shard_map/reduce_scatter | solution.py:338
  558.9 280.8 %reduce-scatter.21.cloned.1.call-start = ((), (), s32[]{:S(2)}) async-start(), calls=%async_computation.19 | async-start | bytes 5898240 | tf_op jit(solution)/shard_map/reduce_scatter | solution.py:332
  566.4 273.3 %copy-start.15 = (f32[2,256]{1,0:T(2,128)S(1)}, f32[2,256]{1,0:T(2,128)}, u32[]{:S(2)}) copy-start(f32[2,256]{1,0:T(2,128)} %get-tuple-element.306) | copy-start | bytes 6148
  566.4 356.9 %all-reduce.23.cloned.1.call-start = ((), (), s32[]{:S(2)}) async-start(), calls=%async_computation.24 | async-start | bytes 7667712 | tf_op jit(solution)/shard_map/psum | solution.py:352
  (23 other events, 88.5 us)
Sparse Core Ops, SparseCore 0:
  9.6 33.6 all-gather.13
  44.9 29.5 all-gather.11
  76.0 29.7 all-gather.9
  107.8 27.9 all-gather.15
  137.3 30.4 all-gather.17
  169.2 88.5 all-gather.19
  259.3 87.8 all-gather.21
  348.7 27.3 all-gather.23
  465.7 36.7 reduce-scatter.14
  505.1 37.9 reduce-scatter.16
  545.3 29.1 reduce-scatter.24
  576.7 27.8 reduce-scatter.26
  607.0 27.8 reduce-scatter.28
  637.6 27.8 reduce-scatter.18
  667.7 83.9 reduce-scatter.22
  753.9 85.7 reduce-scatter.20
  844.3 79.0 all-reduce.22
